TPU v7x, 1024 devices: a whole 4x4x32 slice. The times are simulated.
1024 devices in a mesh: pole: 2 (over z_hi), row: 32 (over x, y, core), col: 16 (over z_lo).
Axes of the slice: x: 4, y: 4, z: 32 (z_hi: 2, z_lo: 16; z = z_hi * 16 + z_lo), core: 2. Of those that a mesh axis runs over, the one named last changes fastest.
Arguments:
- ancestor_inverse: float32 [2, 2, 8192, 8192], P('pole', None, 'col', 'row'), may hold values from -0.0625 to 0.0625
- lower_panel: float32 [2, 2, 8192, 256], P('pole', None, None, 'row'), may hold values from -6 to 6
- pole_weights: float32 [2, 2], P('pole'), may hold values from -1 to 1
- structure: int32 [32, 1], replicated, may hold values 0 or 1
Outputs:
- selected_inverse: float32 [2, 2, 256, 8192], P('pole', None, 'row', 'col')
- density: float32 [256, 8192], P('row')
Inputs may be any that keep to these rules, and one draw needn't show every extreme that they name: 1 where an ancestor supernode lies in a level supernode's structure, else 0.
All inputs are finite; a program needn't handle non-finite values.
Results may differ from a plain program's by a relative error of at most 0.000071.
Values sent between devices are 32-bit elements; how exact they have to be, the bound alone decides.
A program may use at most 32 MiB of HBM per device.

v0:
```python
import jax
import jax.numpy as jnp
from jax import lax
from jax.sharding import PartitionSpec as P

WIDTH = 256


def panel_product(inverse, panel_piece):
    real_part = jnp.einsum(
        "pmk,pkn->npm", inverse[:, 0], panel_piece[:, 0], precision=lax.Precision.HIGHEST
    ) - jnp.einsum(
        "pmk,pkn->npm", inverse[:, 1], panel_piece[:, 1], precision=lax.Precision.HIGHEST
    )
    imaginary = jnp.einsum(
        "pmk,pkn->npm", inverse[:, 0], panel_piece[:, 1], precision=lax.Precision.HIGHEST
    ) + jnp.einsum(
        "pmk,pkn->npm", inverse[:, 1], panel_piece[:, 0], precision=lax.Precision.HIGHEST
    )
    return (real_part, imaginary)


def local(ancestor_inverse, lower_panel, pole_weights, structure):
    row_devices = lax.axis_size("row")
    gathered = lax.all_to_all(lower_panel, "row", split_axis=2, concat_axis=3, tiled=True)
    pole_count, parts, row_count, columns = gathered.shape
    inverse_rows = ancestor_inverse.shape[2]
    block_count = row_count // WIDTH
    node_count = columns // WIDTH
    total_blocks = structure.shape[0]
    first_block = lax.axis_index("row") * block_count
    local_structure = lax.dynamic_slice_in_dim(structure, first_block, block_count, 0).astype(
        jnp.float32
    )
    shaped = gathered.reshape(pole_count, parts, block_count, WIDTH, node_count, WIDTH)
    selected = (shaped * local_structure[None, None, :, None, :, None]).reshape(
        pole_count, parts, row_count, columns
    )
    column_share = columns // row_devices
    real_part, imaginary = panel_product(ancestor_inverse, selected)
    summed = lax.psum_scatter(
        jnp.stack((real_part, imaginary), axis=2).reshape(
            lax.axis_size("row") * column_share, pole_count * 2 * inverse_rows
        ),
        "row",
        scatter_dimension=0,
        tiled=True,
    )
    summed = jnp.transpose(summed.reshape(column_share, pole_count, 2, inverse_rows), (1, 2, 0, 3))
    first_column = lax.axis_index("row") * column_share
    column_node = (first_column + jnp.arange(column_share, dtype=jnp.int32)) // WIDTH
    onehot = (column_node[:, None] == jnp.arange(node_count, dtype=jnp.int32)[None, :]).astype(
        jnp.float32
    )
    node_mask = jnp.dot(onehot, structure.astype(jnp.float32).T, precision=lax.Precision.HIGHEST)
    first_ancestor = lax.axis_index("col") * inverse_rows
    ancestor_block = (first_ancestor + jnp.arange(inverse_rows, dtype=jnp.int32)) // WIDTH
    block_onehot = (
        ancestor_block[:, None] == jnp.arange(total_blocks, dtype=jnp.int32)[None, :]
    ).astype(jnp.float32)
    local_mask = jnp.dot(node_mask, block_onehot.T, precision=lax.Precision.HIGHEST)
    selected_inverse = -summed * local_mask[None, None, :, :]
    weighted = jnp.sum(
        pole_weights[:, 0, None, None] * selected_inverse[:, 1]
        + pole_weights[:, 1, None, None] * selected_inverse[:, 0],
        axis=0,
    )
    pole_total = lax.psum(weighted, "pole")
    density = lax.all_gather(pole_total, "col", axis=1, tiled=True)
    return (selected_inverse, density)


def solution(mesh):
    return jax.shard_map(
        local,
        mesh=mesh,
        in_specs=(
            P("pole", None, "col", "row"),
            P("pole", None, None, "row"),
            P("pole", None),
            P(),
        ),
        out_specs=(P("pole", None, "row", "col"), P("row", None)),
        check_vma=False,
    )
```

profile of v0, /device:TPU:6, one launch (start us, length us, event | category | flops | bytes accessed | tf_op | source)
XLA Modules:
  0.0 363.3 jit_solution(10700488583764693789)
XLA Ops:
  7.2 0.0 copy-start.3
  7.2 9.3 %copy.14 = f32[1,2,8192,8]{3,1,0,2:T(2,128)} copy(f32[1,2,8192,8]{2,3,1,0:T(8,128)} %param.5) | data formatting | bytes 1048576 | tf_op args[1]
  16.4 15.6 %reshape.126 = f32[32,1,4096]{2,1,0:T(1,128)} reshape(f32[8192,1,2,8]{3,2,1,0:T(2,128)} %bitcast.42) | data formatting | bytes 1048576
  32.0 16.8 %all-to-all-start = ((f32[32,1,4096]{2,1,0:T(1,128)}), f32[32,1,4096]{2,1,0:T(1,128)S(1)}, u32[]{:S(2)}, u32[]{:S(2)}) async-start(f32[32,1,4096]{2,1,0:T(1,128)} %reshape.126), calls=%async_computation | async-start | bytes 1048576 | tf_op jit(solution)/shard_map/all_to_all | solution.py:25
  48.8 0.0 reduce-scatter.4.cloned.1.call-start
  48.9 0.0 copy-done.3
  48.9 0.6 fusion.23
  49.5 8.7 %all-to-all-done = f32[32,1,4096]{2,1,0:T(1,128)S(1)} async-done(((f32[32,1,4096]{2,1,0:T(1,128)}), f32[32,1,4096]{2,1,0:T(1,128)S(1)}, u32[]{:S(2)}, u32[]{:S(2)}) %all-to-all-start) | async-done | bytes 524320 | tf_op jit(solution)/shard_map/all_to_all | solution.py:25
  58.2 0.5 broadcast.104
  58.7 1.9 reduce
  60.6 0.0 copy-start
  60.6 14.0 %reshape.127 = f32[8192,1,2,8]{3,2,1,0:T(2,128)} reshape(f32[32,4096]{1,0:T(8,128)S(1)} %reduce) | data formatting | bytes 1048576
  74.6 9.2 %copy.15 = f32[1,2,8192,8]{2,3,1,0:T(8,128)S(1)} copy(f32[1,2,8192,8]{3,1,0,2:T(2,128)} %bitcast.41) | data formatting | bytes 1048576 | tf_op jit(solution)/shard_map/all_to_all | solution.py:25
  83.9 0.0 copy-start.2
  83.9 0.7 broadcast_multiply_fusion
  84.6 0.0 copy-done
  84.6 0.6 fusion.4
  85.2 0.6 fusion.6
  85.9 0.6 fusion
  86.5 0.6 fusion.1
  87.2 0.1 pad_maximum_fusion
  87.2 0.3 copy.16
  87.6 1.3 copy.18
  88.9 0.0 reduce-scatter.4.cloned.1.call-update
  89.0 0.0 copy-done.2
  89.0 0.6 fusion.22
  89.5 0.3 fusion.12
  89.8 127.2 %reduce-scatter.4.cloned.1.call-done = f32[8,1024]{1,0:T(8,128)} async-done(((f32[256,1024]{1,0:T(8,128)}), f32[8,1024]{1,0:T(8,128)}) %reduce-scatter.4.cloned.1.call-update) | async-done | bytes 32784
  217.0 0.9 copy.19
  218.0 0.2 copy.17
  218.2 0.0 copy-start.1
  218.2 1.2 fusion.15
  219.4 46.0 %psum.7 = f32[8,512]{1,0:T(8,128)S(1)} all-reduce(f32[8,512]{1,0:T(8,128)S(1)} %fusion.15), channel_id=1, replica_groups=mesh['pole'=2,'row'=32,'col'=16] {'pole'}, use_global_device_ids=true, to_apply=%region_1.2 | all-reduce | flops 4096 | bytes 32768 | tf_op jit(solution)/shard_map/psum | solution.py:68
  265.4 90.3 %all_gather.3 = f32[8,8192]{1,0:T(8,128)S(1)} all-gather(f32[8,512]{1,0:T(8,128)S(1)} %psum.7), channel_id=1, replica_groups=mesh['pole'=2,'row'=32,'col'=16] {'col'}, dimensions={1}, use_global_device_ids=true | all-gather | bytes 278528 | tf_op jit(solution)/shard_map/all_gather | solution.py:69
  355.8 0.7 copy.21
  356.5 0.0 copy-done.1
  (5 shorter events, 0.1 us)
Async XLA Ops:
  7.2 41.7 %copy-start.3 = (s32[32,1]{0,1:T(1,128)S(1)}, s32[32,1]{0,1:T(1,128)}, u32[]{:S(2)}) copy-start(s32[32,1]{0,1:T(1,128)} %param.7) | copy-start | bytes 388
  32.0 26.1 %all-to-all-start = ((f32[32,1,4096]{2,1,0:T(1,128)}), f32[32,1,4096]{2,1,0:T(1,128)S(1)}, u32[]{:S(2)}, u32[]{:S(2)}) async-start(f32[32,1,4096]{2,1,0:T(1,128)} %reshape.126), calls=%async_computation | async-start | bytes 1048576 | tf_op jit(solution)/shard_map/all_to_all | solution.py:25
  48.8 168.2 %reduce-scatter.4.cloned.1.call-start = ((), (), s32[]{:S(2)}) async-start(), calls=%async_computation.2 | async-start | bytes 1081344
  60.6 24.0 %copy-start = (f32[1,2,512,256]{3,2,1,0:T(8,128)S(1)}, f32[1,2,512,256]{3,2,1,0:T(8,128)}, u32[]{:S(2)}) copy-start(f32[1,2,512,256]{3,2,1,0:T(8,128)} %param.4) | copy-start | bytes 3145732
  83.9 5.1 %copy-start.2 = (f32[1,2]{1,0:T(1,128)S(1)}, f32[1,2]{1,0:T(1,128)}, u32[]{:S(2)}) copy-start(f32[1,2]{1,0:T(1,128)} %param.6) | copy-start | bytes 28
  218.2 138.3 %copy-start.1 = (f32[1,2,8,512]{3,2,1,0:T(8,128)}, f32[1,2,8,512]{3,2,1,0:T(8,128)S(1)}, u32[]{:S(2)}) copy-start(f32[1,2,8,512]{3,2,1,0:T(8,128)S(1)} %multiply_bitcast_fusion) | copy-start | bytes 98308
Sparse Core Ops, SparseCore 0:
  89.0 127.9 reduce-scatter.3
where the time goes:
time: 365 us; the launch traced here: 363 us
  waiting for transfers between devices  136 us (37%)
  blocking collectives  136 us (37%)
  local copies, waits for them, and re-layouts  52.7 us (14%)
  starting transfers between devices  16.9 us (5%)
  between operations  14.2 us (4%)
  other arithmetic  4.53 us (1%)
    unnamed x2, waiting for transfers between devices  127 us
    all_gather x1, blocking collectives, local(): density = lax.all_gather(pole_total, 'col', axis=1, tiled=True)  90.3 us
    psum x1, blocking collectives, local(): pole_total = lax.psum(weighted, 'pole')  46 us
    unnamed x14, local copies, waits for them, and re-layouts  41.9 us
    all_to_all x1, starting transfers between devices, local(): lax.all_to_all(lower_panel, 'row', split_axis=2, concat_axis=3, tiled=True)  16.8 us
    all_to_all x2, local copies, waits for them, and re-layouts, local(): lax.all_to_all(lower_panel, 'row', split_axis=2, concat_axis=3, tiled=True)  9.75 us
    all_to_all x1, waiting for transfers between devices, local(): lax.all_to_all(lower_panel, 'row', split_axis=2, concat_axis=3, tiled=True)  8.66 us
  transfers between devices with their start and end apart: 2, of which 2 were waited for; matrix products, arithmetic and copies ran while one was open for 0% of the time, Pallas kernels for 0%

commit v1 on v0

v1 whole, which is shorter than its diff:
```python
import jax
import jax.numpy as jnp
from jax import lax
from jax.experimental import pallas as pl
from jax.experimental.pallas import tpu as pltpu
from jax.sharding import PartitionSpec as P

MESH = pl.DeviceIdType.MESH
CHIPS = 16
SIDE = 4
DEPTH = 32
COLS = 16
SHARE = 8
K = 256
N = 512
NEAR = (-1, 1, 2)


def split(x):
    high = x.astype(jnp.bfloat16)
    return high, (x - high.astype(jnp.float32)).astype(jnp.bfloat16)


def product(left, right):
    dims = (((1,), (1,)), ((), ()))
    return lax.dot_general(left, right, dims, preferred_element_type=jnp.float32)


def kernel(
    a_hbm, panel_hbm, weights_hbm, structure_hbm, selected_ref, density_ref,
    a_ref, panel_ref, weights_ref, structure_ref, a_high, a_low, s_ref,
    give, keep, got, part, far, pair, chosen,
    load_sem, panel_send, panel_recv, core_send, core_recv, part_send, part_recv,
    far_send, far_recv, near_send, near_recv, store_sem, reach4, reach8,
):
    row = lax.axis_index("row")
    col = lax.axis_index("col")
    z = lax.axis_index("pole") * COLS + col
    chip = lax.div(row, 2)
    core = lax.rem(row, 2)
    x, y = lax.div(chip, SIDE), lax.rem(chip, SIDE)

    def plane(i):
        dx, dy = lax.div(i, SIDE) + 2, lax.rem(i, SIDE) + 2
        return lax.rem(x + dx, SIDE) * SIDE + lax.rem(y + dy, SIDE)

    def along(step):
        other = lax.rem(z + (step % DEPTH), DEPTH)
        return {"pole": lax.div(other, COLS), "col": lax.rem(other, COLS)}

    loads = [
        pltpu.make_async_copy(panel_hbm, panel_ref, load_sem.at[0]),
        pltpu.make_async_copy(a_hbm, a_ref, load_sem.at[1]),
        pltpu.make_async_copy(structure_hbm, structure_ref, load_sem.at[2]),
        pltpu.make_async_copy(weights_hbm, weights_ref, load_sem.at[3]),
    ]
    for load in loads:
        load.start()

    barrier = pltpu.get_barrier_semaphore()
    for step in (-4, 4, -2, 2, -1, 1):
        pl.semaphore_signal(barrier, inc=1, device_id=along(step), device_id_type=MESH)

    own = 2 * CHIPS // 2 + 2 * 2

    def greet(i, _):
        there = plane(lax.div(i, 2)) * 2 + lax.rem(core + lax.rem(i, 2), 2)
        pl.semaphore_signal(barrier, inc=1, device_id={"row": there}, device_id_type=MESH)
        return 0

    lax.fori_loop(0, own, greet, 0)
    lax.fori_loop(own + 1, 2 * CHIPS, greet, 0)
    for load in loads:
        load.wait()
    pl.semaphore_wait(barrier, 2 * CHIPS - 1 + 6)

    def send_panel(i, _):
        there = plane(lax.div(i, 2)) * 2 + lax.rem(core + lax.rem(i, 2), 2)
        pltpu.make_async_remote_copy(
            src_ref=panel_ref.at[:, :, pl.ds(pl.multiple_of(there * K, K), K)],
            dst_ref=s_ref.at[:, core, chip],
            send_sem=panel_send,
            recv_sem=panel_recv,
            device_id={"row": there},
            device_id_type=MESH,
        ).start()
        return 0

    lax.fori_loop(0, own, send_panel, 0)
    lax.fori_loop(own + 1, 2 * CHIPS, send_panel, 0)
    for step in (-4, 4):
        pl.semaphore_signal(reach4, inc=1, device_id=along(step), device_id_type=MESH)

    s_ref[:, core, chip] = panel_ref[:, :, pl.ds(pl.multiple_of(row * K, K), K)]
    row_mask = structure_ref[0, row].astype(jnp.float32)
    high, low = split(a_ref[...] * row_mask)
    a_high[...] = high
    a_low[...] = low

    arrived = panel_ref.at[:, :, pl.ds(0, (2 * CHIPS - 1) * K)]
    pltpu.make_async_copy(arrived, arrived, panel_recv).wait()
    pl.semaphore_wait(reach4, 2)
    for step in (-8, 8):
        pl.semaphore_signal(reach8, inc=1, device_id=along(step), device_id_type=MESH)

    def multiply(which, out):
        parts = []
        for c in range(2):
            parts.append(split(s_ref[c, which].reshape(CHIPS * SHARE, K)))

        def full(s, c):
            return (
                product(s[0], a_high[c]) + product(s[1], a_high[c]) + product(s[0], a_low[c])
            )

        real = full(parts[0], 0) - full(parts[1], 1)
        out[0] = real.reshape(CHIPS, SHARE, N)
        imag = full(parts[1], 0) + full(parts[0], 1)
        out[1] = imag.reshape(CHIPS, SHARE, N)

    multiply(1 - core, give)
    to_core = pltpu.make_async_remote_copy(
        src_ref=give, dst_ref=got, send_sem=core_send, recv_sem=core_recv,
        device_id={"row": chip * 2 + 1 - core}, device_id_type=MESH,
    )
    to_core.start()
    multiply(core, keep)
    to_core.wait_recv()
    keep[...] += got[...]

    mine = CHIPS // 2 + 2

    def send_part(i, _):
        there = plane(i)
        pltpu.make_async_remote_copy(
            src_ref=keep.at[:, there],
            dst_ref=part.at[chip],
            send_sem=part_send,
            recv_sem=part_recv,
            device_id={"row": there * 2 + core},
            device_id_type=MESH,
        ).start()
        return 0

    lax.fori_loop(0, mine, send_part, 0)
    lax.fori_loop(mine + 1, CHIPS, send_part, 0)
    part[chip] = keep[:, chip]
    pltpu.make_async_copy(part.at[pl.ds(1, CHIPS - 1)], part.at[pl.ds(1, CHIPS - 1)], part_recv).wait()

    total = part[0]
    for i in range(1, CHIPS):
        total = total + part[i]
    first = -structure_ref[0, 2 * col].astype(jnp.float32)
    second = -structure_ref[0, 2 * col + 1].astype(jnp.float32)
    chosen[:, :, : N // 2] = total[:, :, : N // 2] * first
    chosen[:, :, N // 2 :] = total[:, :, N // 2 :] * second
    far[0] = weights_ref[0, 0] * chosen[1] + weights_ref[0, 1] * chosen[0]
    pl.semaphore_wait(reach8, 2)
    for m in (4, 3, 5, 2, 6, 1, 7):
        pltpu.make_async_remote_copy(
            src_ref=far.at[0], dst_ref=far.at[8 - m], send_sem=far_send, recv_sem=far_recv,
            device_id=along(4 * m), device_id_type=MESH,
        ).start()
    store = pltpu.make_async_copy(chosen, selected_ref, store_sem.at[0])
    store.start()
    pltpu.make_async_copy(far.at[pl.ds(1, 7)], far.at[pl.ds(1, 7)], far_recv).wait()
    for k in range(4):
        pair[k] = far[k] + far[k + 4]
    for k in range(4):
        place = density_ref.at[:, pl.ds(pl.multiple_of(lax.rem(col + 4 * k, COLS) * N, N), N)]
        for step in NEAR:
            pltpu.make_async_remote_copy(
                src_ref=pair.at[k], dst_ref=place, send_sem=near_send, recv_sem=near_recv,
                device_id=along(step), device_id_type=MESH,
            ).start()
        pltpu.make_async_copy(pair.at[k], place, store_sem.at[1]).start()

    store.wait()
    pltpu.make_async_copy(pair, pair, store_sem.at[1]).wait()
    three = density_ref.at[:, pl.ds(0, 12 * N)]
    pltpu.make_async_copy(three, three, near_recv).wait()
    pltpu.make_async_copy(arrived, arrived, panel_send).wait()
    to_core.wait_send()
    pltpu.make_async_copy(part.at[pl.ds(1, CHIPS - 1)], part.at[pl.ds(1, CHIPS - 1)], part_send).wait()
    pltpu.make_async_copy(far.at[pl.ds(1, 7)], far.at[pl.ds(1, 7)], far_send).wait()
    pltpu.make_async_copy(three, three, near_send).wait()


def local(ancestor_inverse, lower_panel, pole_weights, structure):
    f32, bf16 = jnp.float32, jnp.bfloat16
    dma = pltpu.SemaphoreType.DMA
    selected, density = pl.pallas_call(
        kernel,
        name="level_panel",
        out_shape=(
            jax.ShapeDtypeStruct((2, SHARE, N), f32),
            jax.ShapeDtypeStruct((SHARE, COLS * N), f32),
        ),
        in_specs=[pl.BlockSpec(memory_space=pl.ANY)] * 4,
        out_specs=[pl.BlockSpec(memory_space=pl.ANY)] * 2,
        scratch_shapes=[
            pltpu.VMEM((2, N, K), f32),
            pltpu.VMEM((2, SHARE, 2 * CHIPS * K), f32),
            pltpu.SMEM((1, 2), f32),
            pltpu.SMEM((1, 32), jnp.int32),
            pltpu.VMEM((2, N, K), bf16),
            pltpu.VMEM((2, N, K), bf16),
            pltpu.VMEM((2, 2, CHIPS, SHARE, K), f32),
            pltpu.VMEM((2, CHIPS, SHARE, N), f32),
            pltpu.VMEM((2, CHIPS, SHARE, N), f32),
            pltpu.VMEM((2, CHIPS, SHARE, N), f32),
            pltpu.VMEM((CHIPS, 2, SHARE, N), f32),
            pltpu.VMEM((8, SHARE, N), f32),
            pltpu.VMEM((4, SHARE, N), f32),
            pltpu.VMEM((2, SHARE, N), f32),
            dma((4,)), dma, dma, dma, dma, dma, dma, dma, dma, dma, dma, dma((2,)),
            pltpu.SemaphoreType.REGULAR, pltpu.SemaphoreType.REGULAR,
        ],
        compiler_params=pltpu.CompilerParams(
            collective_id=0, has_side_effects=True, vmem_limit_bytes=60 * 1024 * 1024
        ),
        cost_estimate=pl.CostEstimate(
            flops=3 * 8 * N * K * 256, bytes_accessed=4 << 20, transcendentals=0
        ),
    )(
        ancestor_inverse[0],
        jnp.swapaxes(lower_panel[0], 1, 2),
        pole_weights,
        structure.T,
    )
    return selected[None], density


def solution(mesh):
    return jax.shard_map(
        local,
        mesh=mesh,
        in_specs=(
            P("pole", None, "col", "row"),
            P("pole", None, None, "row"),
            P("pole", None),
            P(),
        ),
        out_specs=(P("pole", None, "row", "col"), P("row", None)),
        check_vma=False,
    )
```

time: 365 us -> 70.2 us (0.19)
  the two profiles are of different devices: /device:TPU:6 before, /device:TPU:2 now
where the time goes in v1:
time: 70.2 us; the launch traced here: 69.9 us
  Pallas kernels  66.2 us (94%)
  local copies, waits for them, and re-layouts  3.04 us (4%)
    pallas_call x1, Pallas kernels, local(): pl.pallas_call(kernel, name='level_panel', out_shape=(jax.ShapeDtypeStruc...  66.2 us
    unnamed x2, local copies, waits for them, and re-layouts  3.04 us

profile of v1, /device:TPU:2, one launch (start us, length us, event | category | flops | bytes accessed | tf_op | source)
XLA Modules:
  0.0 69.9 jit_solution(1674892419037472625)
XLA Ops:
  0.6 66.2 %level_panel.1 = (f32[2,8,512]{2,1,0:T(8,128)}, f32[8,8192]{1,0:T(8,128)}) custom-call(f32[2,512,256]{2,1,0:T(8,128)} %bitcast.7, f32[2,8,8192]{2,1,0:T(8,128)} %bitcast.8, f32[1,2]{1,0:T(1,128)} %weights_hbm.1, s32[1,32]{1,0:T(1,128)} %bitcast.9), custom_call_target="tpu_custom_call" | custom-call | flops 805306368 | bytes 4194304 | tf_op jit(solution)/shard_map/level_panel/pallas_call | solution.py:192
  66.9 1.4 %copy.8 = f32[1,2,8,512]{3,2,1,0:T(8,128)} copy(f32[1,2,8,512]{3,2,1,0:T(8,128)} %bitcast.6) | data formatting | bytes 65536
  68.3 1.7 %copy.9 = f32[8,8192]{1,0:T(8,128)} copy(f32[8,8192]{1,0:T(8,128)} %get-tuple-element.9) | data formatting | bytes 524288

commit v2 on v1

v2 whole, which is shorter than its diff:
```python
import jax
import jax.numpy as jnp
from jax import lax
from jax.experimental import pallas as pl
from jax.experimental.pallas import tpu as pltpu
from jax.sharding import PartitionSpec as P

MESH = pl.DeviceIdType.MESH
CHIPS = 16
SIDE = 4
DEPTH = 32
COLS = 16
BLOCK = 4
SHIFT = 2
HOLDERS = 8
SHARE = 8
K = 256
N = 512


def split(x):
    high = x.astype(jnp.bfloat16)
    return high, (x - high.astype(jnp.float32)).astype(jnp.bfloat16)


def product(left, right):
    dims = (((1,), (1,)), ((), ()))
    return lax.dot_general(left, right, dims, preferred_element_type=jnp.float32)


def full(left, right):
    return product(left[0], right[0]) + product(left[1], right[0]) + product(left[0], right[1])


def kernel(
    a_hbm, panel_hbm, weights_hbm, structure_hbm, selected_ref, density_ref,
    a_ref, panel_ref, weights_ref, structure_ref, a_high, a_low, b_high, b_low, s_ref,
    give, keep, got, part, give_d, keep_d, got_d, part_d, far, pair,
    load_sem, panel_send, panel_recv, core_send, core_recv, part_send, part_recv,
    core_send_d, core_recv_d, part_send_d, part_recv_d,
    far_send, far_recv, near_send, near_recv, reach4, reach8,
):
    row = lax.axis_index("row")
    pole = lax.axis_index("pole")
    col = lax.axis_index("col")
    z = pole * COLS + col
    chip = lax.div(row, 2)
    core = lax.rem(row, 2)
    x, y = lax.div(chip, SIDE), lax.rem(chip, SIDE)
    shifted = lax.rem(z + SHIFT, DEPTH)
    block, member = lax.div(shifted, BLOCK), lax.rem(shifted, BLOCK)

    def plane(i):
        dx, dy = lax.div(i, SIDE) + 2, lax.rem(i, SIDE) + 2
        return lax.rem(x + dx, SIDE) * SIDE + lax.rem(y + dy, SIDE)

    def ring(other):
        other = lax.rem(other, DEPTH)
        return {"pole": lax.div(other, COLS), "col": lax.rem(other, COLS)}

    loads = [
        pltpu.make_async_copy(panel_hbm, panel_ref, load_sem.at[0]),
        pltpu.make_async_copy(a_hbm, a_ref, load_sem.at[1]),
        pltpu.make_async_copy(structure_hbm, structure_ref, load_sem.at[2]),
        pltpu.make_async_copy(weights_hbm, weights_ref, load_sem.at[3]),
    ]
    for load in loads:
        load.start()

    barrier = pltpu.get_barrier_semaphore()
    own = 2 * CHIPS // 2 + 2 * 2

    def greet(i, _):
        there = plane(lax.div(i, 2)) * 2 + lax.rem(core + lax.rem(i, 2), 2)
        pl.semaphore_signal(barrier, inc=1, device_id={"row": there}, device_id_type=MESH)
        return 0

    lax.fori_loop(0, own, greet, 0)
    lax.fori_loop(own + 1, 2 * CHIPS, greet, 0)
    for step in (1, 2, BLOCK):
        for other in (z + step, z + DEPTH - step):
            pl.semaphore_signal(barrier, inc=1, device_id=ring(other), device_id_type=MESH)
    for load in loads:
        load.wait()
    pl.semaphore_wait(barrier, 2 * CHIPS - 1 + 6)

    def send_panel(i, _):
        there = plane(lax.div(i, 2)) * 2 + lax.rem(core + lax.rem(i, 2), 2)
        pltpu.make_async_remote_copy(
            src_ref=panel_ref.at[:, :, pl.ds(pl.multiple_of(there * K, K), K)],
            dst_ref=s_ref.at[:, core, chip],
            send_sem=panel_send,
            recv_sem=panel_recv,
            device_id={"row": there},
            device_id_type=MESH,
        ).start()
        return 0

    lax.fori_loop(0, own, send_panel, 0)
    lax.fori_loop(own + 1, 2 * CHIPS, send_panel, 0)
    for step in (BLOCK, DEPTH - BLOCK):
        pl.semaphore_signal(reach4, inc=1, device_id=ring(z + step), device_id_type=MESH)

    s_ref[:, core, chip] = panel_ref[:, :, pl.ds(pl.multiple_of(row * K, K), K)]
    row_mask = structure_ref[0, row].astype(jnp.float32)
    w_real, w_imag = weights_ref[0, 0], weights_ref[0, 1]
    a_real, a_imag = a_ref[0] * row_mask, a_ref[1] * row_mask
    b_high[0], b_low[0] = split(w_imag * a_real + w_real * a_imag)
    b_high[1], b_low[1] = split(w_real * a_real - w_imag * a_imag)
    a_high[0], a_low[0] = split(a_real)
    a_high[1], a_low[1] = split(a_imag)
    pl.semaphore_wait(reach4, 2)
    for step in (2 * BLOCK, DEPTH - 2 * BLOCK):
        pl.semaphore_signal(reach8, inc=1, device_id=ring(z + step), device_id_type=MESH)

    arrived = panel_ref.at[:, :, pl.ds(0, (2 * CHIPS - 1) * K)]
    pltpu.make_async_copy(arrived, arrived, panel_recv).wait()

    def pieces(which):
        return [split(s_ref[c, which].reshape(CHIPS * SHARE, K)) for c in range(2)]

    def multiply_d(which, out):
        s = pieces(which)
        value = full(s[0], (b_high[0], b_low[0])) + full(s[1], (b_high[1], b_low[1]))
        out[...] = value.reshape(CHIPS, SHARE, N)

    def multiply(which, out):
        s = pieces(which)
        real, imag = (a_high[0], a_low[0]), (a_high[1], a_low[1])
        out[0] = (full(s[0], real) - full(s[1], imag)).reshape(CHIPS, SHARE, N)
        out[1] = (full(s[1], real) + full(s[0], imag)).reshape(CHIPS, SHARE, N)

    def to_core(source, target, send, recv):
        return pltpu.make_async_remote_copy(
            src_ref=source, dst_ref=target, send_sem=send, recv_sem=recv,
            device_id={"row": chip * 2 + 1 - core}, device_id_type=MESH,
        )

    mine = CHIPS // 2 + 2

    def spread(take, target, send, recv):
        def send_part(i, _):
            there = plane(i)
            pltpu.make_async_remote_copy(
                src_ref=take(there), dst_ref=target.at[chip], send_sem=send, recv_sem=recv,
                device_id={"row": there * 2 + core}, device_id_type=MESH,
            ).start()
            return 0

        lax.fori_loop(0, mine, send_part, 0)
        lax.fori_loop(mine + 1, CHIPS, send_part, 0)

    def rest(ref):
        return ref.at[pl.ds(1, CHIPS - 1)]

    def total(ref):
        value = ref[0]
        for i in range(1, CHIPS):
            value = value + ref[i]
        return value

    multiply_d(1 - core, give_d)
    core_copy_d = to_core(give_d, got_d, core_send_d, core_recv_d)
    core_copy_d.start()
    multiply_d(core, keep_d)
    core_copy_d.wait_recv()
    keep_d[...] += got_d[...]
    spread(lambda there: keep_d.at[there], part_d, part_send_d, part_recv_d)
    part_d[chip] = keep_d[chip]
    multiply(1 - core, give)
    core_copy = to_core(give, got, core_send, core_recv)
    core_copy.start()
    pltpu.make_async_copy(rest(part_d), rest(part_d), part_recv_d).wait()
    first = -structure_ref[0, 2 * col].astype(jnp.float32)
    second = -structure_ref[0, 2 * col + 1].astype(jnp.float32)

    def masked(value):
        half = N // 2
        return jnp.concatenate([value[..., :half] * first, value[..., half:] * second], axis=-1)

    far[block] = masked(total(part_d))

    def send_far(target):
        pltpu.make_async_remote_copy(
            src_ref=far.at[block], dst_ref=far.at[block], send_sem=far_send,
            recv_sem=far_recv.at[block], device_id=ring(target * BLOCK + member + DEPTH - SHIFT),
            device_id_type=MESH,
        ).start()

    def send_far_to(*targets):
        for target in targets:
            pl.when(block != target)(lambda target=target: send_far(target))

    pl.semaphore_wait(reach8, 2)
    send_far_to(0, 1)

    multiply(core, keep)
    send_far_to(2, 3)
    core_copy.wait_recv()
    keep[...] += got[...]
    spread(lambda there: keep.at[:, there], part, part_send, part_recv)
    send_far_to(4, 5, 6, 7)
    part[chip] = keep[:, chip]

    def landed(slot):
        pltpu.make_async_copy(far.at[slot], far.at[slot], far_recv.at[slot]).wait()

    half_ring = HOLDERS // 2
    for step in (2, 1, 3, 0):
        low = lax.rem(block + step, half_ring)
        if step == 0:
            landed(lax.rem(block + half_ring, HOLDERS))
        else:
            landed(low)
            landed(low + half_ring)
        pair[low] = far[low] + far[low + half_ring]
        source = lax.rem(low * BLOCK + member + DEPTH - SHIFT, COLS)
        columns = pl.ds(pl.multiple_of(source * N, N), N)
        place = density_ref.at[:, columns]
        two = 2 + (DEPTH - 4) * (1 - lax.div(lax.rem(low + 1, half_ring), 2))
        for i in (1, DEPTH - 1, two):
            pltpu.make_async_remote_copy(
                src_ref=pair.at[low], dst_ref=place, send_sem=near_send, recv_sem=near_recv,
                device_id=ring(z + i), device_id_type=MESH,
            ).start()
        density_ref[:, columns] = pair[low]

    pltpu.make_async_copy(rest(part), rest(part), part_recv).wait()
    selected_ref[...] = masked(total(part))

    near = density_ref.at[:, pl.ds(0, (COLS - BLOCK) * N)]
    pltpu.make_async_copy(near, near, near_recv).wait()
    pltpu.make_async_copy(arrived, arrived, panel_send).wait()
    core_copy_d.wait_send()
    core_copy.wait_send()
    pltpu.make_async_copy(rest(part_d), rest(part_d), part_send_d).wait()
    pltpu.make_async_copy(rest(part), rest(part), part_send).wait()
    seven = far.at[pl.ds(1, HOLDERS - 1)]
    pltpu.make_async_copy(seven, seven, far_send).wait()
    pltpu.make_async_copy(near, near, near_send).wait()


def finish(selected_in, density_in, selected_out, density_out, sem):
    copies = [
        pltpu.make_async_copy(selected_in, selected_out, sem.at[0]),
        pltpu.make_async_copy(density_in, density_out, sem.at[1]),
    ]
    for copy in copies:
        copy.start()
    for copy in copies:
        copy.wait()


def local(ancestor_inverse, lower_panel, pole_weights, structure):
    f32, bf16 = jnp.float32, jnp.bfloat16
    dma = pltpu.SemaphoreType.DMA
    outputs = ((2, SHARE, N), f32), ((SHARE, COLS * N), f32)
    anywhere = pl.BlockSpec(memory_space=pl.ANY)
    selected, density = pl.pallas_call(
        kernel,
        name="level_panel",
        out_shape=tuple(pltpu.VMEM(*output) for output in outputs),
        in_specs=[anywhere] * 4,
        out_specs=[pl.BlockSpec(memory_space=pltpu.VMEM)] * 2,
        scratch_shapes=[
            pltpu.VMEM((2, N, K), f32),
            pltpu.VMEM((2, SHARE, 2 * CHIPS * K), f32),
            pltpu.SMEM((1, 2), f32),
            pltpu.SMEM((1, 32), jnp.int32),
            pltpu.VMEM((2, N, K), bf16),
            pltpu.VMEM((2, N, K), bf16),
            pltpu.VMEM((2, N, K), bf16),
            pltpu.VMEM((2, N, K), bf16),
            pltpu.VMEM((2, 2, CHIPS, SHARE, K), f32),
            pltpu.VMEM((2, CHIPS, SHARE, N), f32),
            pltpu.VMEM((2, CHIPS, SHARE, N), f32),
            pltpu.VMEM((2, CHIPS, SHARE, N), f32),
            pltpu.VMEM((CHIPS, 2, SHARE, N), f32),
            pltpu.VMEM((CHIPS, SHARE, N), f32),
            pltpu.VMEM((CHIPS, SHARE, N), f32),
            pltpu.VMEM((CHIPS, SHARE, N), f32),
            pltpu.VMEM((CHIPS, SHARE, N), f32),
            pltpu.VMEM((HOLDERS, SHARE, N), f32),
            pltpu.VMEM((HOLDERS // 2, SHARE, N), f32),
            dma((4,)), dma, dma, dma, dma, dma, dma, dma, dma, dma, dma,
            dma, dma((HOLDERS,)), dma, dma,
            pltpu.SemaphoreType.REGULAR, pltpu.SemaphoreType.REGULAR,
        ],
        compiler_params=pltpu.CompilerParams(
            collective_id=0, has_side_effects=True, vmem_limit_bytes=60 * 1024 * 1024
        ),
        cost_estimate=pl.CostEstimate(
            flops=3 * 12 * N * K * 256, bytes_accessed=4 << 20, transcendentals=0
        ),
    )(
        ancestor_inverse[0],
        jnp.swapaxes(lower_panel[0], 1, 2),
        pole_weights,
        structure.T,
    )
    selected, density = pl.pallas_call(
        finish,
        name="store_panels",
        out_shape=tuple(jax.ShapeDtypeStruct(*output) for output in outputs),
        in_specs=[anywhere] * 2,
        out_specs=[anywhere] * 2,
        scratch_shapes=[dma((2,))],
        compiler_params=pltpu.CompilerParams(vmem_limit_bytes=8 * 1024 * 1024),
    )(selected, density)
    return selected[None], density


def solution(mesh):
    return jax.shard_map(
        local,
        mesh=mesh,
        in_specs=(
            P("pole", None, "col", "row"),
            P("pole", None, None, "row"),
            P("pole", None),
            P(),
        ),
        out_specs=(P("pole", None, "row", "col"), P("row", None)),
        check_vma=False,
    )
```

time: 70.2 us -> 60.7 us (0.86)
  Pallas kernels: 66.2 us -> 59.9 us
  local copies, waits for them, and re-layouts: 3.04 us -> 0 us
    pallas_call x1 -> x2, Pallas kernels: 66.2 us -> 59.9 us  [the longest x1 59.2 us: local(): pl.pallas_call(kernel, name='level_panel', out_shape=tuple((pltpu.VMEM(*o...]
    unnamed x2 -> x0, local copies, waits for them, and re-layouts: 3.04 us -> none
where the time goes in v2:
time: 60.7 us; the launch traced here: 60.6 us
  Pallas kernels  59.9 us (99%)
  between operations  0.64 us (1%)
    pallas_call x1, Pallas kernels, local(): pl.pallas_call(kernel, name='level_panel', out_shape=tuple((pltpu.VMEM(*o...  59.2 us

profile of v2, /device:TPU:2, one launch (start us, length us, event | category | flops | bytes accessed | tf_op | source)
XLA Modules:
  0.0 60.6 jit_solution(15217325008625713528)
XLA Ops:
  0.6 59.2 %level_panel.1 = (f32[2,8,512]{2,1,0:T(8,128)S(1)}, f32[8,8192]{1,0:T(8,128)S(1)}) custom-call(f32[2,512,256]{2,1,0:T(8,128)} %bitcast.6, f32[2,8,8192]{2,1,0:T(8,128)} %bitcast.7, f32[1,2]{1,0:T(1,128)} %weights_hbm.1, s32[1,32]{1,0:T(1,128)} %bitcast.9), custom_call_target="tpu_custom_call" | custom-call | flops 1207959552 | bytes 4194304 | tf_op jit(solution)/shard_map/level_panel/pallas_call | solution.py:259
  59.8 0.7 %store_panels.1 = (f32[2,8,512]{2,1,0:T(8,128)}, f32[8,8192]{1,0:T(8,128)}) custom-call(f32[2,8,512]{2,1,0:T(8,128)S(1)} %get-tuple-element.6.selected_in, f32[8,8192]{1,0:T(8,128)S(1)} %get-tuple-element.7.density_in), custom_call_target="tpu_custom_call" | custom-call | tf_op jit(solution)/shard_map/store_panels/pallas_call | solution.py:301

commit v3 on v2

v3 whole, which is shorter than its diff:
```python
import jax
import jax.numpy as jnp
from jax import lax
from jax.experimental import pallas as pl
from jax.experimental.pallas import tpu as pltpu
from jax.sharding import PartitionSpec as P

MESH = pl.DeviceIdType.MESH
CHIPS = 16
SIDE = 4
HALF = 8
OWN = 10
DEPTH = 32
COLS = 16
BLOCK = 4
SHIFT = 2
HOLDERS = 8
SHARE = 8
K = 256
N = 512


def split(x):
    high = x.astype(jnp.bfloat16)
    return high, (x - high.astype(jnp.float32)).astype(jnp.bfloat16)


def product(left, right):
    dims = (((1,), (0,)), ((), ()))
    return lax.dot_general(left, right, dims, preferred_element_type=jnp.float32)


def full(left, right):
    return product(left[0], right[0]) + product(left[1], right[0]) + product(left[0], right[1])


def kernel(
    a_hbm, panel_hbm, weights_hbm, structure_hbm, selected_ref, density_ref,
    a_ref, panel_ref, weights_ref, structure_ref, a_high, a_low, b_high, b_low, s_ref,
    give, keep, got, part, own_d, got_d, part_d, far, pair,
    load_sem, panel_send, panel_recv, core_send, core_recv, part_send, part_recv,
    core_send_d, core_recv_d, part_send_d, part_recv_d,
    far_send, far_recv, near_send, near_recv, reach4, reach8,
):
    row = lax.axis_index("row")
    pole = lax.axis_index("pole")
    col = lax.axis_index("col")
    z = pole * COLS + col
    chip = lax.div(row, 2)
    core = lax.rem(row, 2)
    x, y = lax.div(chip, SIDE), lax.rem(chip, SIDE)
    shifted = lax.rem(z + SHIFT, DEPTH)
    block, member = lax.div(shifted, BLOCK), lax.rem(shifted, BLOCK)
    agent = core == 1

    def plane(slot):
        dx, dy = lax.div(slot, SIDE) + 2, lax.rem(slot, SIDE) + 2
        return lax.rem(x + dx, SIDE) * SIDE + lax.rem(y + dy, SIDE)

    def back(slot):
        dx, dy = SIDE - lax.div(slot, SIDE), SIDE - lax.rem(slot, SIDE)
        return lax.rem(dx, SIDE) * SIDE + lax.rem(dy, SIDE)

    def ring(other, core_there):
        other = lax.rem(other, DEPTH)
        there = {"pole": lax.div(other, COLS), "col": lax.rem(other, COLS)}
        return {**there, "row": chip * 2 + core_there}

    barrier = pltpu.get_barrier_semaphore()

    def greet(i, _):
        there = plane(lax.div(i, 2)) * 2 + lax.rem(core + lax.rem(i, 2), 2)
        pl.semaphore_signal(barrier, inc=1, device_id={"row": there}, device_id_type=MESH)
        return 0

    def greet_along(*steps):
        for step in steps:
            for other in (z + step, z + DEPTH - step):
                pl.semaphore_signal(
                    barrier, inc=1, device_id=ring(other, 1), device_id_type=MESH
                )

    lax.fori_loop(0, 2 * OWN, greet, 0)
    lax.fori_loop(2 * OWN + 1, 2 * CHIPS, greet, 0)
    greet_along(1, 2)
    pl.when(agent)(lambda: greet_along(BLOCK))
    loads = [
        pltpu.make_async_copy(panel_hbm, panel_ref, load_sem.at[0]),
        pltpu.make_async_copy(a_hbm, a_ref, load_sem.at[1]),
        pltpu.make_async_copy(structure_hbm, structure_ref, load_sem.at[2]),
        pltpu.make_async_copy(weights_hbm, weights_ref, load_sem.at[3]),
    ]
    for load in loads:
        load.start()
    for load in loads:
        load.wait()
    pl.semaphore_wait(barrier, 2 * CHIPS - 1 + 10 * core)

    def send_panel(half):
        def send(i, _):
            slot = lax.div(i, 2)
            there = plane(back(slot)) * 2 + lax.rem(core + lax.rem(i, 2), 2)
            pltpu.make_async_remote_copy(
                src_ref=panel_ref.at[:, :, pl.ds(pl.multiple_of(there * K, K), K)],
                dst_ref=s_ref.at[:, slot, core],
                send_sem=panel_send,
                recv_sem=panel_recv.at[half],
                device_id={"row": there},
                device_id_type=MESH,
            ).start()
            return 0

        return send

    lax.fori_loop(0, CHIPS, send_panel(0), 0)
    lax.fori_loop(CHIPS, 2 * OWN, send_panel(1), 0)
    lax.fori_loop(2 * OWN + 1, 2 * CHIPS, send_panel(1), 0)

    def reach(sem, step):
        for other in (z + step, z + DEPTH - step):
            pl.semaphore_signal(sem, inc=1, device_id=ring(other, 1), device_id_type=MESH)

    pl.when(agent)(lambda: reach(reach4, BLOCK))

    s_ref[:, OWN, core] = panel_ref[:, :, pl.ds(pl.multiple_of(row * K, K), K)]
    row_mask = structure_ref[0, row].astype(jnp.float32)
    w_real, w_imag = weights_ref[0, 0], weights_ref[0, 1]
    a_real, a_imag = a_ref[0].T * row_mask, a_ref[1].T * row_mask
    b_high[0], b_low[0] = split(w_imag * a_real + w_real * a_imag)
    b_high[1], b_low[1] = split(w_real * a_real - w_imag * a_imag)
    a_high[0], a_low[0] = split(a_real)
    a_high[1], a_low[1] = split(a_imag)

    @pl.when(agent)
    def _():
        pl.semaphore_wait(reach4, 2)
        reach(reach8, 2 * BLOCK)

    def arrived(half):
        return panel_ref.at[:, :, pl.ds(0, (CHIPS - half) * K)]

    def multiply_d(half):
        pltpu.make_async_copy(arrived(half), arrived(half), panel_recv.at[half]).wait()
        s = []
        for c in range(2):
            rows = s_ref[c, half * HALF : (half + 1) * HALF]
            s.append(split(rows.reshape(CHIPS * SHARE, K)))
        value = full(s[0], (b_high[0], b_low[0])) + full(s[1], (b_high[1], b_low[1]))
        own_d[half * HALF : (half + 1) * HALF] = value.reshape(HALF, 2, SHARE, N)

    def multiply(which, out):
        s = [split(s_ref[c, :, which].reshape(CHIPS * SHARE, K)) for c in range(2)]
        real, imag = (a_high[0], a_low[0]), (a_high[1], a_low[1])
        out[0] = (full(s[0], real) - full(s[1], imag)).reshape(CHIPS, SHARE, N)
        out[1] = (full(s[1], real) + full(s[0], imag)).reshape(CHIPS, SHARE, N)

    def to_core(source, target, send, recv):
        return pltpu.make_async_remote_copy(
            src_ref=source, dst_ref=target, send_sem=send, recv_sem=recv,
            device_id={"row": chip * 2 + 1 - core}, device_id_type=MESH,
        )

    def spread(first, last, take, target, send, recv):
        def send_part(slot, _):
            pltpu.make_async_remote_copy(
                src_ref=take(slot), dst_ref=target.at[back(slot)], send_sem=send,
                recv_sem=recv, device_id={"row": plane(slot) * 2 + core}, device_id_type=MESH,
            ).start()
            return 0

        lax.fori_loop(first, last, send_part, 0)

    def rest(ref):
        return ref.at[pl.ds(1, CHIPS - 1)]

    def total(ref, first_slot=0):
        value = ref[first_slot]
        for i in range(1, CHIPS):
            value = value + ref[first_slot + i]
        return value

    first = -structure_ref[0, 2 * col].astype(jnp.float32)
    second = -structure_ref[0, 2 * col + 1].astype(jnp.float32)

    def masked(value):
        half = N // 2
        return jnp.concatenate([value[..., :half] * first, value[..., half:] * second], axis=-1)

    def spread_d(first, last):
        def send_part(slot, _):
            pltpu.make_async_remote_copy(
                src_ref=own_d.at[slot, core], dst_ref=part_d.at[core * CHIPS + back(slot)],
                send_sem=part_send_d, recv_sem=part_recv_d,
                device_id={"row": plane(slot) * 2 + 1}, device_id_type=MESH,
            ).start()
            return 0

        lax.fori_loop(first, last, send_part, 0)

    halves = []
    for half in range(2):
        slots = pl.ds(half * HALF, HALF)
        multiply_d(half)
        halves.append(
            to_core(
                own_d.at[slots, 1 - core], got_d.at[slots],
                core_send_d.at[half], core_recv_d.at[half],
            )
        )
        halves[half].start()
    for half in range(2):
        slots = pl.ds(half * HALF, HALF)
        halves[half].wait_recv()
        own_d[slots, core] += got_d[slots]
        if half == 0:
            spread_d(0, HALF)
        else:
            spread_d(HALF, OWN)
            spread_d(OWN + 1, CHIPS)
            pl.when(core == 0)(lambda: spread_d(OWN, OWN + 1))
    d_others = part_d.at[pl.ds(1, 2 * CHIPS - 1)]

    multiply(1 - core, give)
    core_copy = to_core(give, got, core_send, core_recv)
    core_copy.start()

    def send_far(target):
        pltpu.make_async_remote_copy(
            src_ref=far.at[block], dst_ref=far.at[block], send_sem=far_send,
            recv_sem=far_recv.at[block],
            device_id=ring(target * BLOCK + member + DEPTH - SHIFT, 1),
            device_id_type=MESH,
        ).start()

    def send_far_to(*targets):
        for target in targets:
            pl.when(agent & (block != target))(lambda target=target: send_far(target))

    @pl.when(agent)
    def _():
        part_d[CHIPS + OWN] = own_d[OWN, 1]
        pltpu.make_async_copy(d_others, d_others, part_recv_d).wait()
        far[block, 0] = masked(total(part_d, 0))
        far[block, 1] = masked(total(part_d, CHIPS))
        pl.semaphore_wait(reach8, 2)

    send_far_to(0, 1)

    multiply(core, keep)
    send_far_to(2, 3)
    core_copy.wait_recv()
    keep[...] += got[...]
    spread(0, OWN, lambda i: keep.at[:, i], part, part_send, part_recv)
    spread(OWN + 1, CHIPS, lambda i: keep.at[:, i], part, part_send, part_recv)
    send_far_to(4, 5, 6, 7)
    part[OWN] = keep[:, OWN]

    def landed(slot):
        pltpu.make_async_copy(far.at[slot], far.at[slot], far_recv.at[slot]).wait()

    half_ring = HOLDERS // 2

    @pl.when(agent)
    def _():
        for step in (2, 1, 3, 0):
            low = lax.rem(block + step, half_ring)
            if step == 0:
                landed(lax.rem(block + half_ring, HOLDERS))
            else:
                landed(low)
                landed(low + half_ring)
            pair[low] = far[low] + far[low + half_ring]
            source = lax.rem(low * BLOCK + member + DEPTH - SHIFT, COLS)
            columns = pl.ds(pl.multiple_of(source * N, N), N)
            two = 2 + (DEPTH - 4) * (1 - lax.div(lax.rem(low + 1, half_ring), 2))
            for core_there, steps in ((0, (1, DEPTH - 1, two)), (1, (1, DEPTH - 1, two)), (0, (0,))):
                for i in steps:
                    pltpu.make_async_remote_copy(
                        src_ref=pair.at[low, core_there], dst_ref=density_ref.at[:, columns],
                        send_sem=near_send, recv_sem=near_recv,
                        device_id=ring(z + i, core_there), device_id_type=MESH,
                    ).start()
            density_ref[:, columns] = pair[low, 1]

    pltpu.make_async_copy(rest(part), rest(part), part_recv).wait()
    selected_ref[...] = masked(total(part))

    panel_sent = panel_ref.at[:, :, pl.ds(0, (2 * CHIPS - 1) * K)]
    pltpu.make_async_copy(panel_sent, panel_sent, panel_send).wait()
    for half in range(2):
        halves[half].wait_send()
    core_copy.wait_send()
    pltpu.make_async_copy(rest(part), rest(part), part_send).wait()

    @pl.when(core == 0)
    def _():
        pltpu.make_async_copy(got_d, got_d, part_send_d).wait()
        pltpu.make_async_copy(density_ref, density_ref, near_recv).wait()

    @pl.when(agent)
    def _():
        pltpu.make_async_copy(rest(got_d), rest(got_d), part_send_d).wait()
        seven = far.at[pl.ds(1, HOLDERS - 1)]
        pltpu.make_async_copy(seven, seven, far_send).wait()
        near = density_ref.at[:, pl.ds(0, (COLS - BLOCK) * N)]
        pltpu.make_async_copy(near, near, near_recv).wait()
        sent = part_d.at[pl.ds(0, 28)]
        pltpu.make_async_copy(sent, sent, near_send).wait()


def finish(selected_in, density_in, selected_out, density_out, sem):
    copies = [
        pltpu.make_async_copy(selected_in, selected_out, sem.at[0]),
        pltpu.make_async_copy(density_in, density_out, sem.at[1]),
    ]
    for copy in copies:
        copy.start()
    for copy in copies:
        copy.wait()


def local(ancestor_inverse, lower_panel, pole_weights, structure):
    f32, bf16 = jnp.float32, jnp.bfloat16
    dma = pltpu.SemaphoreType.DMA
    outputs = ((2, SHARE, N), f32), ((SHARE, COLS * N), f32)
    anywhere = pl.BlockSpec(memory_space=pl.ANY)
    selected, density = pl.pallas_call(
        kernel,
        name="level_panel",
        out_shape=tuple(pltpu.VMEM(*output) for output in outputs),
        in_specs=[anywhere] * 4,
        out_specs=[pl.BlockSpec(memory_space=pltpu.VMEM)] * 2,
        scratch_shapes=[
            pltpu.VMEM((2, N, K), f32),
            pltpu.VMEM((2, SHARE, 2 * CHIPS * K), f32),
            pltpu.SMEM((1, 2), f32),
            pltpu.SMEM((1, 32), jnp.int32),
            pltpu.VMEM((2, K, N), bf16),
            pltpu.VMEM((2, K, N), bf16),
            pltpu.VMEM((2, K, N), bf16),
            pltpu.VMEM((2, K, N), bf16),
            pltpu.VMEM((2, CHIPS, 2, SHARE, K), f32),
            pltpu.VMEM((2, CHIPS, SHARE, N), f32),
            pltpu.VMEM((2, CHIPS, SHARE, N), f32),
            pltpu.VMEM((2, CHIPS, SHARE, N), f32),
            pltpu.VMEM((CHIPS, 2, SHARE, N), f32),
            pltpu.VMEM((CHIPS, 2, SHARE, N), f32),
            pltpu.VMEM((CHIPS, SHARE, N), f32),
            pltpu.VMEM((2 * CHIPS, SHARE, N), f32),
            pltpu.VMEM((HOLDERS, 2, SHARE, N), f32),
            pltpu.VMEM((HOLDERS // 2, 2, SHARE, N), f32),
            dma((4,)), dma, dma((2,)), dma, dma, dma, dma, dma((2,)), dma((2,)), dma, dma,
            dma, dma((HOLDERS,)), dma, dma,
            pltpu.SemaphoreType.REGULAR, pltpu.SemaphoreType.REGULAR,
        ],
        compiler_params=pltpu.CompilerParams(
            collective_id=0, has_side_effects=True, vmem_limit_bytes=60 * 1024 * 1024
        ),
        cost_estimate=pl.CostEstimate(
            flops=3 * 12 * N * K * 256, bytes_accessed=4 << 20, transcendentals=0
        ),
    )(
        ancestor_inverse[0],
        jnp.swapaxes(lower_panel[0], 1, 2),
        pole_weights,
        structure.T,
    )
    selected, density = pl.pallas_call(
        finish,
        name="store_panels",
        out_shape=tuple(jax.ShapeDtypeStruct(*output) for output in outputs),
        in_specs=[anywhere] * 2,
        out_specs=[anywhere] * 2,
        scratch_shapes=[dma((2,))],
        compiler_params=pltpu.CompilerParams(vmem_limit_bytes=8 * 1024 * 1024),
    )(selected, density)
    return selected[None], density


def solution(mesh):
    return jax.shard_map(
        local,
        mesh=mesh,
        in_specs=(
            P("pole", None, "col", "row"),
            P("pole", None, None, "row"),
            P("pole", None),
            P(),
        ),
        out_specs=(P("pole", None, "row", "col"), P("row", None)),
        check_vma=False,
    )
```

time: 60.7 us -> 59.9 us (0.987)
  the two profiles are of different devices: /device:TPU:2 before, /device:TPU:33 now
where the time goes in v3:
time: 59.9 us; the launch traced here: 59.7 us
  Pallas kernels  59 us (98%)
  between operations  0.64 us (1%)
    pallas_call x1, Pallas kernels, local(): pl.pallas_call(kernel, name='level_panel', out_shape=tuple((pltpu.VMEM(*o...  58.3 us

profile of v3, /device:TPU:33, one launch (start us, length us, event | category | flops | bytes accessed | tf_op | source)
XLA Modules:
  0.0 59.7 jit_solution(2630732529617243009)
XLA Ops:
  0.6 58.3 %level_panel.1 = (f32[2,8,512]{2,1,0:T(8,128)S(1)}, f32[8,8192]{1,0:T(8,128)S(1)}) custom-call(f32[2,512,256]{2,1,0:T(8,128)} %bitcast.6, f32[2,8,8192]{2,1,0:T(8,128)} %bitcast.7, f32[1,2]{1,0:T(1,128)} %weights_hbm.1, s32[1,32]{1,0:T(1,128)} %bitcast.9), custom_call_target="tpu_custom_call" | custom-call | flops 1207959552 | bytes 4194304 | tf_op jit(solution)/shard_map/level_panel/pallas_call | solution.py:327
  59.0 0.7 %store_panels.1 = (f32[2,8,512]{2,1,0:T(8,128)}, f32[8,8192]{1,0:T(8,128)}) custom-call(f32[2,8,512]{2,1,0:T(8,128)S(1)} %get-tuple-element.6.selected_in, f32[8,8192]{1,0:T(8,128)S(1)} %get-tuple-element.7.density_in), custom_call_target="tpu_custom_call" | custom-call | tf_op jit(solution)/shard_map/store_panels/pallas_call | solution.py:368

commit v4 on v3

--- a/solution.py
+++ b/solution.py
@@ -54,12 +54,11 @@
     agent = core == 1
 
     def plane(slot):
-        dx, dy = lax.div(slot, SIDE) + 2, lax.rem(slot, SIDE) + 2
+        dx, dy = slot // SIDE + 2, slot % SIDE + 2
         return lax.rem(x + dx, SIDE) * SIDE + lax.rem(y + dy, SIDE)
 
     def back(slot):
-        dx, dy = SIDE - lax.div(slot, SIDE), SIDE - lax.rem(slot, SIDE)
-        return lax.rem(dx, SIDE) * SIDE + lax.rem(dy, SIDE)
+        return (SIDE - slot // SIDE) % SIDE * SIDE + (SIDE - slot % SIDE) % SIDE
 
     def ring(other, core_there):
         other = lax.rem(other, DEPTH)
@@ -68,10 +67,9 @@
 
     barrier = pltpu.get_barrier_semaphore()
 
-    def greet(i, _):
-        there = plane(lax.div(i, 2)) * 2 + lax.rem(core + lax.rem(i, 2), 2)
+    def greet(i):
+        there = plane(i // 2) * 2 + lax.rem(core + i % 2, 2)
         pl.semaphore_signal(barrier, inc=1, device_id={"row": there}, device_id_type=MESH)
-        return 0
 
     def greet_along(*steps):
         for step in steps:
@@ -80,8 +78,9 @@
                     barrier, inc=1, device_id=ring(other, 1), device_id_type=MESH
                 )
 
-    lax.fori_loop(0, 2 * OWN, greet, 0)
-    lax.fori_loop(2 * OWN + 1, 2 * CHIPS, greet, 0)
+    for i in range(2 * CHIPS):
+        if i != 2 * OWN:
+            greet(i)
     greet_along(1, 2)
     pl.when(agent)(lambda: greet_along(BLOCK))
     loads = [
@@ -96,25 +95,21 @@
         load.wait()
     pl.semaphore_wait(barrier, 2 * CHIPS - 1 + 10 * core)
 
-    def send_panel(half):
-        def send(i, _):
-            slot = lax.div(i, 2)
-            there = plane(back(slot)) * 2 + lax.rem(core + lax.rem(i, 2), 2)
-            pltpu.make_async_remote_copy(
-                src_ref=panel_ref.at[:, :, pl.ds(pl.multiple_of(there * K, K), K)],
-                dst_ref=s_ref.at[:, slot, core],
-                send_sem=panel_send,
-                recv_sem=panel_recv.at[half],
-                device_id={"row": there},
-                device_id_type=MESH,
-            ).start()
-            return 0
-
-        return send
-
-    lax.fori_loop(0, CHIPS, send_panel(0), 0)
-    lax.fori_loop(CHIPS, 2 * OWN, send_panel(1), 0)
-    lax.fori_loop(2 * OWN + 1, 2 * CHIPS, send_panel(1), 0)
+    def send_panel(i):
+        slot = i // 2
+        there = plane(back(slot)) * 2 + lax.rem(core + i % 2, 2)
+        pltpu.make_async_remote_copy(
+            src_ref=panel_ref.at[:, :, pl.ds(pl.multiple_of(there * K, K), K)],
+            dst_ref=s_ref.at[:, slot, core],
+            send_sem=panel_send,
+            recv_sem=panel_recv.at[slot // HALF],
+            device_id={"row": there},
+            device_id_type=MESH,
+        ).start()
+
+    for i in range(2 * CHIPS):
+        if i != 2 * OWN:
+            send_panel(i)
 
     def reach(sem, step):
         for other in (z + step, z + DEPTH - step):

time: 59.9 us -> 60 us (level)
  no operation moved by 1% of the time
where the time goes in v4:
time: 60 us; the launch traced here: 59.9 us
  Pallas kernels  59.2 us (99%)
  between operations  0.64 us (1%)
    pallas_call x1, Pallas kernels, local(): pl.pallas_call(kernel, name='level_panel', out_shape=tuple((pltpu.VMEM(*o...  58.5 us

profile of v4, /device:TPU:33, one launch (start us, length us, event | category | flops | bytes accessed | tf_op | source)
XLA Modules:
  0.0 59.9 jit_solution(6203353238776518950)
XLA Ops:
  0.6 58.5 %level_panel.1 = (f32[2,8,512]{2,1,0:T(8,128)S(1)}, f32[8,8192]{1,0:T(8,128)S(1)}) custom-call(f32[2,512,256]{2,1,0:T(8,128)} %bitcast.6, f32[2,8,8192]{2,1,0:T(8,128)} %bitcast.7, f32[1,2]{1,0:T(1,128)} %weights_hbm.1, s32[1,32]{1,0:T(1,128)} %bitcast.9), custom_call_target="tpu_custom_call" | custom-call | flops 1207959552 | bytes 4194304 | tf_op jit(solution)/shard_map/level_panel/pallas_call | solution.py:322
  59.1 0.7 %store_panels.1 = (f32[2,8,512]{2,1,0:T(8,128)}, f32[8,8192]{1,0:T(8,128)}) custom-call(f32[2,8,512]{2,1,0:T(8,128)S(1)} %get-tuple-element.6.selected_in, f32[8,8192]{1,0:T(8,128)S(1)} %get-tuple-element.7.density_in), custom_call_target="tpu_custom_call" | custom-call | tf_op jit(solution)/shard_map/store_panels/pallas_call | solution.py:363
